TPU v7x, 512 devices: a whole 4x8x8 slice. The times are simulated.
512 devices in a mesh: seq: 64 (over y, x, core), chan: 8 (over z).
Axes of the slice: x: 4, y: 8, z: 8, core: 2. Of those that a mesh axis runs over, the one named last changes fastest.
Arguments:
- hidden_in: bfloat16 [8192, 8192], P('seq', 'chan'), as said below
- query_mr: bfloat16 [8192, 8192], P('seq', 'chan'), may hold values from -6 to 6
- key_mr: bfloat16 [8192, 8192], P('seq', 'chan'), may hold values from -6 to 6
- value_mr: bfloat16 [8192, 8192], P('seq', 'chan'), may hold values from -6 to 6
- query_li: bfloat16 [8192, 8192], P('seq', 'chan'), may hold values from -6 to 6
- key_li: bfloat16 [8192, 8192], P('seq', 'chan'), may hold values from -6 to 6
- mr_filter: bfloat16 [128, 512], P(None, 'chan'), may hold values from -0.5 to 0.5
- li_rate: float32 [16, 8192], P(None, 'chan'), as said below
- li_residue: float32 [16, 8192], P(None, 'chan'), may hold values from -4 to 4
- norm_gain: float32 [8192], P('chan'), may hold values from 0.25 to 1.75
Outputs:
- normed_out: bfloat16 [8192, 8192], P('seq', 'chan')
Inputs may be any that keep to these rules, and one draw needn't show every extreme that they name: `hidden_in`: real values of moderate size. `li_rate`: decay rates per position, all positive, from 1 / 81920 to 1 / 30.
All inputs are finite; a program needn't handle non-finite values.
Results may differ from a plain program's by a relative error of at most 0.0055.
Values may be sent and summed in bfloat16 or wider, within the bound.
No kernel may reach another device: no remote copies, remote signals or barrier semaphores. Data moves between devices by JAX's collectives and lax.ppermute only.
A program may use at most 64 MiB of HBM per device.

v0:
```python
import jax
import jax.numpy as jnp
from jax import lax
from jax.sharding import PartitionSpec as P


def passed_along(block, axis, distance):
    devices = range(lax.axis_size(axis))
    route = [(i - distance, i) for i in devices if i - distance in devices]
    return lax.ppermute(block, axis, route)


def band_matrix(filter_taps, filter_len):
    group_count = filter_taps.shape[1]
    padded = jnp.concatenate(
        [
            jnp.zeros((1, group_count), filter_taps.dtype),
            jnp.flip(filter_taps, 0),
            jnp.zeros((filter_len, group_count), filter_taps.dtype),
        ],
        0,
    )
    repeated = jnp.tile(padded, (filter_len, 1))[: filter_len * 2 * filter_len]
    return repeated.reshape(filter_len, 2 * filter_len, group_count)


def band_apply(toeplitz, earlier, latter, group_count):
    rows, channels = earlier.shape
    filter_len = toeplitz.shape[0]
    blocks = rows // filter_len
    earlier_rows = earlier.reshape(blocks, filter_len, group_count, channels // group_count)
    latter_rows = latter.reshape(blocks, filter_len, group_count, channels // group_count)
    windows = jnp.concatenate([earlier_rows, latter_rows], 1)
    result = jnp.einsum("tsg,bsgk->btgk", toeplitz, windows, preferred_element_type=jnp.float32)
    return result.reshape(rows, channels)


def per_device(
    hidden_in,
    query_mr,
    key_mr,
    value_mr,
    query_li,
    key_li,
    mr_filter,
    li_rate,
    li_residue,
    norm_gain,
):
    tokens, channels = key_mr.shape
    filter_len = mr_filter.shape[0]
    group_count = mr_filter.shape[1]
    highest = lax.Precision.HIGHEST
    product = (key_mr.astype(jnp.float32) * value_mr.astype(jnp.float32)).astype(jnp.bfloat16)
    toeplitz = band_matrix(mr_filter, filter_len)
    prior_rows = passed_along(product[tokens - filter_len + 1 :], "seq", 1)
    first_earlier = jnp.concatenate([jnp.zeros((1, channels), jnp.bfloat16), prior_rows], 0)
    earlier_all = jnp.concatenate([first_earlier, product[: tokens - filter_len]], 0)
    conv_mr = band_apply(toeplitz, earlier_all, product, group_count)
    out_mr = (query_mr.astype(jnp.float32) * conv_mr).astype(jnp.bfloat16)
    source = key_li.astype(jnp.float32) * out_mr.astype(jnp.float32)
    block_len = 16
    block_count = tokens // block_len
    scaled = li_residue * jnp.sqrt(-jnp.expm1(-2.0 * li_rate))
    lag_steps = jnp.arange(block_len).astype(jnp.float32)
    mode_taps = jnp.sum(scaled[None] * jnp.exp(-lag_steps[:, None, None] * li_rate[None]), 1)
    lag_index = jnp.arange(block_len)
    lag_grid = lag_index[:, None] - lag_index[None, :]
    selector = (lag_grid[:, :, None] == lag_index[None, None, :]).astype(jnp.float32)
    intra_block = jnp.einsum("tsd,dc->tsc", selector, mode_taps, precision=highest)
    decay_out = jnp.exp(-(block_len - 1 - lag_steps)[:, None, None] * li_rate[None])
    decay_in = scaled[None] * jnp.exp(-(lag_steps + 1.0)[:, None, None] * li_rate[None])
    blocks_in = source.reshape(block_count, block_len, channels)
    local_part = jnp.einsum("tsc,bsc->btc", intra_block, blocks_in, precision=highest)
    block_ends = jnp.einsum("snc,bsc->bnc", decay_out, blocks_in, precision=highest)
    block_decay = jnp.exp(-block_len * li_rate)

    def combine_blocks(earlier, latter):
        return (earlier[0] * latter[0], latter[0] * earlier[1] + latter[1])

    _, inclusive = lax.associative_scan(
        combine_blocks, (jnp.broadcast_to(block_decay[None], block_ends.shape), block_ends), axis=0
    )
    position = lax.axis_index("seq")
    shard_rows = lax.all_gather(inclusive[-1:], "seq", axis=0, tiled=True)
    owners = jnp.arange(shard_rows.shape[0], dtype=jnp.int32)
    distance = jnp.maximum(position - 1 - owners, 0).astype(jnp.float32)
    weight = jnp.where(
        (owners < position)[:, None, None],
        jnp.exp(-(tokens * distance)[:, None, None] * li_rate[None]),
        0.0,
    )
    incoming = jnp.sum(weight * shard_rows, 0)
    offsets = jnp.arange(block_count).astype(jnp.float32) * block_len
    start_states = (
        jnp.concatenate([jnp.zeros_like(inclusive[:1]), inclusive[:-1]], 0)
        + jnp.exp(-offsets[:, None, None] * li_rate[None]) * incoming[None]
    )
    from_states = jnp.einsum("tnc,bnc->btc", decay_in, start_states, precision=highest)
    conv_li = (local_part + from_states).reshape(tokens, channels)
    combined = (
        hidden_in.astype(jnp.float32)
        + out_mr.astype(jnp.float32)
        + query_li.astype(jnp.float32) * conv_li
    )
    local_squares = jnp.sum(combined * combined, axis=1)
    square_sum = lax.psum(local_squares, "chan")
    inverse_rms = lax.rsqrt(square_sum / (channels * lax.axis_size("chan")) + 1e-06)
    return (combined * inverse_rms[:, None] * norm_gain[None, :]).astype(jnp.bfloat16)


def solution(mesh):
    in_specs = (
        P("seq", "chan"),
        P("seq", "chan"),
        P("seq", "chan"),
        P("seq", "chan"),
        P("seq", "chan"),
        P("seq", "chan"),
        P(None, "chan"),
        P(None, "chan"),
        P(None, "chan"),
        P("chan"),
    )
    out_specs = P("seq", "chan")
    return jax.shard_map(
        per_device, mesh=mesh, in_specs=in_specs, out_specs=out_specs, check_vma=False
    )
```

profile of v0, /device:TPU:16, one launch (start us, length us, event | category | flops | bytes accessed | tf_op | source)
XLA Modules:
  0.0 193.9 jit_solution(13816346787504282258)
XLA Ops:
  6.5 1.1 multiply_convert_fusion.2
  7.7 1.9 collective-permute-start
  9.6 0.8 rev.4
  10.6 0.2 copy.99
  10.8 3.2 %tile.4 = bf16[128,257,64]{1,0,2:T(8,128)(2,1)} broadcast(bf16[257,64]{0,1:T(8,128)(2,1)S(1)} %maximum_maximum_fusion), dimensions={1,2} | broadcast | bytes 4243584 | tf_op jit(solution)/shard_map/tile | solution.py:23
  14.0 10.8 %tile.10 = bf16[32896,64]{0,1:T(8,128)(2,1)} reshape(bf16[128,257,64]{1,0,2:T(8,128)(2,1)} %tile.4) | data formatting | bytes 8421376 | tf_op jit(solution)/shard_map/tile | solution.py:23
  24.8 2.2 %slice-done = bf16[32768,64]{0,1:T(8,128)(2,1)S(1)} async-done(((bf16[32896,64]{0,1:T(8,128)(2,1)}), bf16[32768,64]{0,1:T(8,128)(2,1)S(1)}, s32[]{:S(2)}) %slice-start) | async-done | bytes 4194328 | tf_op jit(solution)/shard_map/slice | solution.py:23
  27.0 3.0 %copy.113 = bf16[8,8,128,256]{3,2,1,0:T(8,128)(2,1)} copy(bf16[8,8,128,256]{3,1,2,0:T(8,128)(2,1)S(1)} %bitcast.43) | data formatting | bytes 8388608
  30.1 0.2 copy.102
  30.4 0.2 copy.112
  30.7 3.4 %fusion.15 = f32[64,16,128]{2,1,0:T(8,128)S(1)} fusion(bf16[128,256,64]{1,0,2:T(8,128)(2,1)} %bitcast.44, bf16[1,128,64,16]{1,3,2,0:T(8,128)(2,1)S(1)} %bitcast.51, bf16[1,128,64,16]{1,3,2,0:T(8,128)(2,1)S(1)} %bitcast.50), kind=kOutput, calls=%fused_computation.19 | convolution fusion | flops 68157440 | bytes 5242880 | tf_op jit(solution)/shard_map/tsg,bsgk->btgk/dot_general | solution.py:34
  34.1 0.2 copy.100
  34.4 2.6 %copy.104 = f32[8,16,1024]{1,0,2:T(8,128)} copy(f32[8,16,1024]{2,1,0:T(8,128)S(1)} %bitcast.48) | data formatting | bytes 1048576 | tf_op jit(solution)/shard_map/reshape | solution.py:73
  37.1 11.1 %fusion.4 = f32[1024,8,16]{2,1,0:T(8,128)} fusion(f32[8,16,1024]{1,0,2:T(8,128)} %copy.104, f32[16]{0:T(128)S(1)} %subtract_negate_fusion, f32[16,1024]{0,1:T(8,128)S(1)} %copy.102), kind=kOutput, calls=%fused_computation.4 | convolution fusion | flops 25427968 | bytes 1114176 | tf_op jit(solution)/shard_map/snc,bsc->bnc/dot_general | solution.py:75
  48.1 2.8 %copy.107 = f32[1024,8,16]{0,2,1:T(8,128)S(1)} copy(f32[1024,8,16]{2,1,0:T(8,128)} %fusion.4) | data formatting | bytes 1048576 | tf_op jit(solution)/shard_map/snc,bsc->bnc/dot_general | solution.py:75
  51.3 0.6 slice.129
  52.0 0.2 copy.101
  52.2 3.5 %multiply_reduce_fusion = f32[16,1024]{0,1:T(8,128)S(1)} fusion(f32[16,1024]{0,1:T(8,128)S(1)} %copy.102, f32[16]{0:T(128)S(1)} %convert_negate_fusion, f32[16,1024]{0,1:T(8,128)S(1)} %copy.101), kind=kLoop, calls=%fused_computation.7 | loop fusion | flops 770048 | bytes 196672 | tf_op jit(solution)/shard_map/reduce_sum | solution.py:66
  55.7 0.6 fusion.18
  56.3 6.2 %copy.105 = f32[16,16,1024]{1,0,2:T(8,128)} copy(f32[16,16,1024]{2,1,0:T(8,128)S(1)} %fusion.18) | data formatting | bytes 2097152 | tf_op jit(solution)/shard_map/tsd,dc->tsc/dot_general | solution.py:70
  62.5 0.2 pad.26
  62.8 1.0 fusion.20
  63.9 17.5 %fusion.29 = f32[1024,8,16]{2,1,0:T(8,128)} fusion(f32[8,16,1024]{1,0,2:T(8,128)} %copy.104, f32[16,16,1024]{1,0,2:T(8,128)} %copy.105), kind=kOutput, calls=%fused_computation.62 | convolution fusion | flops 25165824 | bytes 2097152 | tf_op jit(solution)/shard_map/tsc,bsc->btc/dot_general | solution.py:74
  81.4 60.2 %all-gather.2.cloned.1.call-done = f32[64,16,1024]{2,1,0:T(8,128)} async-done(((f32[1,16,1024]{2,1,0:T(8,128)}), f32[64,16,1024]{2,1,0:T(8,128)}) %all-gather.2.cloned.1.call-update) | async-done | bytes 4194320 | tf_op jit(solution)/shard_map/all_gather | solution.py:85
  141.6 3.1 %multiply_reduce_fusion.1 = f32[16,1024]{1,0:T(8,128)S(1)} fusion(f32[64,16,1024]{2,1,0:T(8,128)} %all-gather.2.cloned.1.call-done, f32[16,1024]{1,0:T(8,128)S(1)} %copy-done, f32[64]{0:T(128)S(1)} %multiply_negate_fusion, pred[64]{0:T(512)(128)(4,1)S(1)} %iota_compare_fusion.2), kind=kLoop, calls=%fused_computation.10 | loop fusion | flops 4177920 | bytes 4325696 | tf_op jit(solution)/shard_map/reduce_sum | solution.py:93
  144.7 0.2 multiply_add_fusion
  144.9 2.6 %copy.108 = f32[8,16,1024]{1,0,2:T(8,128)} copy(f32[8,16,1024]{2,1,0:T(8,128)S(1)} %multiply_add_fusion) | data formatting | bytes 1048576 | tf_op jit(solution)/shard_map/add | solution.py:96
  147.5 17.5 %add_bitcast_fusion = f32[8,16,1024]{1,0,2:T(8,128)} fusion(f32[1024,8,16]{2,1,0:T(8,128)} %fusion.29, f32[8,16,1024]{1,0,2:T(8,128)} %copy.108, f32[16]{0:T(128)S(1)} %add_negate_fusion, f32[16,1024]{0,1:T(8,128)S(1)} %copy.102, f32[16,1024]{0,1:T(8,128)S(1)} %copy.101), kind=kOutput, calls=%fused_computation.8 | convolution fusion | flops 25821184 | bytes 1704000 | tf_op jit(solution)/shard_map/tnc,bnc->btc/dot_general | solution.py:99
  165.0 2.9 %copy.109 = f32[8,16,1024]{2,1,0:T(8,128)S(1)} copy(f32[8,16,1024]{1,0,2:T(8,128)} %add_bitcast_fusion) | data formatting | bytes 1048576 | tf_op jit(solution)/shard_map/add | solution.py:100
  167.9 0.2 multiply_reduce_fusion.2
  168.1 18.1 %psum.7 = f32[128]{0:T(128)S(1)} all-reduce(f32[128]{0:T(128)S(1)} %multiply_reduce_fusion.2), channel_id=1, replica_groups=mesh['seq'=64,'chan'=8] {'chan'}, use_global_device_ids=true, to_apply=%region_3.4 | all-reduce | flops 128 | bytes 1024 | tf_op jit(solution)/shard_map/psum | solution.py:107
  186.2 0.9 multiply_convert_fusion
  (50 shorter events, 1.1 us)
Async XLA Ops:
  6.5 135.0 %all-gather.2.cloned.1.call-start = ((), (), s32[]{:S(2)}) async-start(), calls=%async_computation | async-start | bytes 4259840 | tf_op jit(solution)/shard_map/all_gather | solution.py:85
  7.7 22.6 %collective-permute-start = (bf16[127,1024]{1,0:T(8,128)(2,1)S(1)}, bf16[127,1024]{1,0:T(8,128)(2,1)S(1)}, u32[]{:S(2)}, u32[]{:S(2)}) collective-permute-start(bf16[127,1024]{1,0:T(8,128)(2,1)S(1)} %slice.90), channel_id=1, source_target_pairs={{0,8},{8,16},{16,24},{24,32},{32,40},{40,48},{48,56},{56,64},{64,7... | collective-permute-start | bytes 780296 | tf_op jit(solution)/shard_map/ppermute | solution.py:10
  24.8 2.2 %slice-start = ((bf16[32896,64]{0,1:T(8,128)(2,1)}), bf16[32768,64]{0,1:T(8,128)(2,1)S(1)}, s32[]{:S(2)}) async-start(bf16[32896,64]{0,1:T(8,128)(2,1)} %tile.10), calls=%async_computation.1 | async-start | bytes 8388608 | tf_op jit(solution)/shard_map/slice | solution.py:23
  27.0 3.0 %copy-start = (f32[16,1024]{1,0:T(8,128)S(1)}, f32[16,1024]{1,0:T(8,128)}, u32[]{:S(2)}) copy-start(f32[16,1024]{1,0:T(8,128)} %param.17) | copy-start | bytes 196612
  27.0 3.2 %copy-start.6 = (f32[16,1024]{1,0:T(8,128)S(1)}, f32[16,1024]{1,0:T(8,128)}, u32[]{:S(2)}) copy-start(f32[16,1024]{1,0:T(8,128)} %param.18) | copy-start | bytes 196612
  30.1 4.2 %copy-start.4 = (bf16[128,1024]{1,0:T(8,128)(2,1)S(1)}, bf16[128,1024]{1,0:T(8,128)(2,1)}, u32[]{:S(2)}) copy-start(bf16[128,1024]{1,0:T(8,128)(2,1)} %param.15) | copy-start | bytes 786436
  30.1 4.2 %copy-start.5 = (bf16[128,1024]{1,0:T(8,128)(2,1)S(1)}, bf16[128,1024]{1,0:T(8,128)(2,1)}, u32[]{:S(2)}) copy-start(bf16[128,1024]{1,0:T(8,128)(2,1)} %param.11) | copy-start | bytes 786436
  51.2 0.8 copy-start.1
  165.0 2.9 %copy-start.2 = (bf16[128,1024]{1,0:T(8,128)(2,1)S(1)}, bf16[128,1024]{1,0:T(8,128)(2,1)}, u32[]{:S(2)}) copy-start(bf16[128,1024]{1,0:T(8,128)(2,1)} %param.14) | copy-start | bytes 786436
  165.0 2.9 %copy-start.3 = (bf16[128,1024]{1,0:T(8,128)(2,1)S(1)}, bf16[128,1024]{1,0:T(8,128)(2,1)}, u32[]{:S(2)}) copy-start(bf16[128,1024]{1,0:T(8,128)(2,1)} %param.10) | copy-start | bytes 786436
  165.0 21.2 %copy-start.7 = (f32[1024]{0:T(1024)S(1)}, f32[1024]{0:T(1024)}, u32[]{:S(2)}) copy-start(f32[1024]{0:T(1024)} %param.19) | copy-start | bytes 12292
Sparse Core Ops, SparseCore 0:
  52.1 89.4 all-gather.1
where the time goes:
time: 194 us
  waiting for transfers between devices  60.2 us (31%)
  matrix products  50 us (26%)
  local copies, waits for them, and re-layouts  39.5 us (20%)
  blocking collectives  18.1 us (9%)
  between operations  13.7 us (7%)
  other arithmetic  10.4 us (5%)
    all_gather x1, waiting for transfers between devices, per_device(): shard_rows = lax.all_gather(inclusive[-1:], 'seq', axis=0, tiled=True)  60.2 us
    psum x1, blocking collectives, per_device(): square_sum = lax.psum(local_squares, 'chan')  18.1 us
    dot_general x1, matrix products, per_device(): jnp.einsum('tnc,bnc->btc', decay_in, start_states, precision=highest)  17.5 us
    dot_general x1, matrix products, per_device(): jnp.einsum('tsc,bsc->btc', intra_block, blocks_in, precision=highest)  17.5 us
    another operation x2, local copies, waits for them, and re-layouts, band_matrix(): repeated = jnp.tile(padded, (filter_len, 1))[:filter_len * 2 * filter_len]  14 us
    dot_general x1, matrix products, per_device(): jnp.einsum('snc,bsc->bnc', decay_out, blocks_in, precision=highest)  11.1 us
    dot_general x1, local copies, waits for them, and re-layouts, per_device(): jnp.einsum('tsd,dc->tsc', selector, mode_taps, precision=highest)  6.16 us
  transfers between devices with their start and end apart: 2, of which 1 were waited for; matrix products, arithmetic and copies ran while one was open for 25% of the time, Pallas kernels for 0%

commit v1 on v0

--- a/solution.py
+++ b/solution.py
@@ -82,7 +82,9 @@
         combine_blocks, (jnp.broadcast_to(block_decay[None], block_ends.shape), block_ends), axis=0
     )
     position = lax.axis_index("seq")
-    shard_rows = lax.all_gather(inclusive[-1:], "seq", axis=0, tiled=True)
+    shard_rows = jnp.concatenate(
+        lax.all_to_all(jnp.stack([inclusive[-1:]] * lax.axis_size("seq")), "seq", 0, 0), axis=0
+    )
     owners = jnp.arange(shard_rows.shape[0], dtype=jnp.int32)
     distance = jnp.maximum(position - 1 - owners, 0).astype(jnp.float32)
     weight = jnp.where(

time: 194 us -> 206 us (1.062)
  the two profiles are of different devices: /device:TPU:16 before, /device:TPU:2 now
where the time goes in v1:
time: 206 us
  waiting for transfers between devices  66.9 us (32%)
  matrix products  50 us (24%)
  local copies, waits for them, and re-layouts  41.1 us (20%)
  blocking collectives  23.2 us (11%)
  starting transfers between devices  13.7 us (7%)
  other arithmetic  10.5 us (5%)
    all_to_all x1, waiting for transfers between devices, per_device(): lax.all_to_all(jnp.stack([inclusive[-1:]] * lax.axis_size('seq')), 'seq',...  66.9 us
    psum x1, blocking collectives, per_device(): square_sum = lax.psum(local_squares, 'chan')  23.2 us
    dot_general x1, matrix products, per_device(): jnp.einsum('tnc,bnc->btc', decay_in, start_states, precision=highest)  17.5 us
    dot_general x1, matrix products, per_device(): jnp.einsum('tsc,bsc->btc', intra_block, blocks_in, precision=highest)  17.4 us
    another operation x2, local copies, waits for them, and re-layouts, band_matrix(): repeated = jnp.tile(padded, (filter_len, 1))[:filter_len * 2 * filter_len]  14 us
    all_to_all x1, starting transfers between devices, per_device(): lax.all_to_all(jnp.stack([inclusive[-1:]] * lax.axis_size('seq')), 'seq',...  11.8 us
    dot_general x1, matrix products, per_device(): jnp.einsum('snc,bsc->bnc', decay_out, blocks_in, precision=highest)  11.1 us
    dot_general x1, local copies, waits for them, and re-layouts, per_device(): jnp.einsum('tsd,dc->tsc', selector, mode_taps, precision=highest)  6.15 us
  transfers between devices with their start and end apart: 2, of which 1 were waited for; matrix products, arithmetic and copies ran while one was open for 23% of the time, Pallas kernels for 0%

profile of v1, /device:TPU:2, one launch (start us, length us, event | category | flops | bytes accessed | tf_op | source)
XLA Modules:
  0.0 205.7 jit_solution(9429715464677841002)
XLA Ops:
  0.0 1.1 multiply_convert_fusion.2
  1.2 1.9 collective-permute-start
  3.1 0.8 rev.4
  4.1 0.2 copy.99
  4.3 3.2 %tile.4 = bf16[128,257,64]{1,0,2:T(8,128)(2,1)} broadcast(bf16[257,64]{0,1:T(8,128)(2,1)S(1)} %maximum_maximum_fusion), dimensions={1,2} | broadcast | bytes 4243584 | tf_op jit(solution)/shard_map/tile | solution.py:23
  7.5 10.8 %tile.10 = bf16[32896,64]{0,1:T(8,128)(2,1)} reshape(bf16[128,257,64]{1,0,2:T(8,128)(2,1)} %tile.4) | data formatting | bytes 8421376 | tf_op jit(solution)/shard_map/tile | solution.py:23
  18.3 2.2 %slice-done = bf16[32768,64]{0,1:T(8,128)(2,1)S(1)} async-done(((bf16[32896,64]{0,1:T(8,128)(2,1)}), bf16[32768,64]{0,1:T(8,128)(2,1)S(1)}, s32[]{:S(2)}) %slice-start) | async-done | bytes 4194328 | tf_op jit(solution)/shard_map/slice | solution.py:23
  20.5 3.0 %copy.113 = bf16[8,8,128,256]{3,2,1,0:T(8,128)(2,1)} copy(bf16[8,8,128,256]{3,1,2,0:T(8,128)(2,1)S(1)} %bitcast.49) | data formatting | bytes 8388608
  23.5 0.2 copy.102
  23.8 0.2 copy.112
  24.1 3.4 %fusion.16 = f32[64,16,128]{2,1,0:T(8,128)S(1)} fusion(bf16[128,256,64]{1,0,2:T(8,128)(2,1)} %bitcast.50, bf16[1,128,64,16]{1,3,2,0:T(8,128)(2,1)S(1)} %bitcast.57, bf16[1,128,64,16]{1,3,2,0:T(8,128)(2,1)S(1)} %bitcast.56), kind=kOutput, calls=%fused_computation.20 | convolution fusion | flops 68157440 | bytes 5242880 | tf_op jit(solution)/shard_map/tsg,bsgk->btgk/dot_general | solution.py:34
  27.5 0.2 copy.100
  27.9 2.6 %copy.104 = f32[8,16,1024]{1,0,2:T(8,128)} copy(f32[8,16,1024]{2,1,0:T(8,128)S(1)} %bitcast.54) | data formatting | bytes 1048576 | tf_op jit(solution)/shard_map/reshape | solution.py:73
  30.5 11.1 %fusion.4 = f32[1024,8,16]{2,1,0:T(8,128)} fusion(f32[8,16,1024]{1,0,2:T(8,128)} %copy.104, f32[16]{0:T(128)S(1)} %subtract_negate_fusion, f32[16,1024]{0,1:T(8,128)S(1)} %copy.102), kind=kOutput, calls=%fused_computation.4 | convolution fusion | flops 25427968 | bytes 1114176 | tf_op jit(solution)/shard_map/snc,bsc->bnc/dot_general | solution.py:75
  41.6 2.8 %copy.107 = f32[1024,8,16]{0,2,1:T(8,128)S(1)} copy(f32[1024,8,16]{2,1,0:T(8,128)} %fusion.4) | data formatting | bytes 1048576 | tf_op jit(solution)/shard_map/snc,bsc->bnc/dot_general | solution.py:75
  44.7 2.5 %stack.2 = f32[64,1,16,1024]{3,2,1,0:T(8,128)} broadcast(f32[16,1024]{1,0:T(8,128)S(1)} %add_bitcast_fusion.1), dimensions={2,3} | broadcast | bytes 4259840 | tf_op jit(solution)/shard_map/stack | solution.py:86
  47.2 11.8 %all-to-all-start = ((f32[64,1,16,1024]{3,2,1,0:T(8,128)}), f32[64,1,16,1024]{3,2,1,0:T(8,128)}, u32[]{:S(2)}, u32[]{:S(2)}) async-start(f32[64,1,16,1024]{3,2,1,0:T(8,128)} %stack.2), calls=%async_computation | async-start | bytes 8388608 | tf_op jit(solution)/shard_map/all_to_all | solution.py:86
  59.0 0.2 copy.101
  59.2 3.5 %multiply_reduce_fusion = f32[16,1024]{0,1:T(8,128)S(1)} fusion(f32[16,1024]{0,1:T(8,128)S(1)} %copy.102, f32[16]{0:T(128)S(1)} %convert_negate_fusion, f32[16,1024]{0,1:T(8,128)S(1)} %copy.101), kind=kLoop, calls=%fused_computation.7 | loop fusion | flops 770048 | bytes 196672 | tf_op jit(solution)/shard_map/reduce_sum | solution.py:66
  62.7 0.6 fusion.19
  63.4 6.2 %copy.105 = f32[16,16,1024]{1,0,2:T(8,128)} copy(f32[16,16,1024]{2,1,0:T(8,128)S(1)} %fusion.19) | data formatting | bytes 2097152 | tf_op jit(solution)/shard_map/tsd,dc->tsc/dot_general | solution.py:70
  69.6 1.0 fusion.21
  70.8 17.4 %fusion.30 = f32[1024,8,16]{2,1,0:T(8,128)} fusion(f32[8,16,1024]{1,0,2:T(8,128)} %copy.104, f32[16,16,1024]{1,0,2:T(8,128)} %copy.105), kind=kOutput, calls=%fused_computation.64 | convolution fusion | flops 25165824 | bytes 2097152 | tf_op jit(solution)/shard_map/tsc,bsc->btc/dot_general | solution.py:74
  88.2 66.9 %all-to-all-done = f32[64,1,16,1024]{3,2,1,0:T(8,128)} async-done(((f32[64,1,16,1024]{3,2,1,0:T(8,128)}), f32[64,1,16,1024]{3,2,1,0:T(8,128)}, u32[]{:S(2)}, u32[]{:S(2)}) %all-to-all-start) | async-done | bytes 4194336 | tf_op jit(solution)/shard_map/all_to_all | solution.py:86
  155.1 3.1 %fusion.7 = f32[16,1024]{1,0:T(8,128)S(1)} fusion(f32[64,1,16,1024]{3,2,1,0:T(8,128)} %all-to-all-done, f32[16,1024]{1,0:T(8,128)S(1)} %copy-done, f32[64]{0:T(128)S(1)} %multiply_negate_fusion, pred[64]{0:T(512)(128)(4,1)S(1)} %iota_compare_fusion.2), kind=kLoop, calls=%fused_computation.9 | loop fusion | flops 4177920 | bytes 4325696 | tf_op jit(solution)/shard_map/reduce_sum | solution.py:95
  158.3 0.2 multiply_add_fusion
  158.4 2.6 %copy.108 = f32[8,16,1024]{1,0,2:T(8,128)} copy(f32[8,16,1024]{2,1,0:T(8,128)S(1)} %multiply_add_fusion) | data formatting | bytes 1048576 | tf_op jit(solution)/shard_map/add | solution.py:98
  161.0 17.5 %add_bitcast_fusion = f32[8,16,1024]{1,0,2:T(8,128)} fusion(f32[1024,8,16]{2,1,0:T(8,128)} %fusion.30, f32[8,16,1024]{1,0,2:T(8,128)} %copy.108, f32[16]{0:T(128)S(1)} %add_negate_fusion, f32[16,1024]{0,1:T(8,128)S(1)} %copy.102, f32[16,1024]{0,1:T(8,128)S(1)} %copy.101), kind=kOutput, calls=%fused_computation.10 | convolution fusion | flops 25821184 | bytes 1704000 | tf_op jit(solution)/shard_map/tnc,bnc->btc/dot_general | solution.py:101
  178.5 2.9 %copy.109 = f32[8,16,1024]{2,1,0:T(8,128)S(1)} copy(f32[8,16,1024]{1,0,2:T(8,128)} %add_bitcast_fusion) | data formatting | bytes 1048576 | tf_op jit(solution)/shard_map/add | solution.py:102
  181.4 0.2 multiply_reduce_fusion.1
  181.6 23.2 %psum.7 = f32[128]{0:T(128)S(1)} all-reduce(f32[128]{0:T(128)S(1)} %multiply_reduce_fusion.1), channel_id=1, replica_groups=mesh['seq'=64,'chan'=8] {'chan'}, use_global_device_ids=true, to_apply=%region_3.4 | all-reduce | flops 128 | bytes 1024 | tf_op jit(solution)/shard_map/psum | solution.py:109
  204.8 0.9 multiply_convert_fusion
  (50 shorter events, 1.1 us)
Async XLA Ops:
  1.2 22.6 %collective-permute-start = (bf16[127,1024]{1,0:T(8,128)(2,1)S(1)}, bf16[127,1024]{1,0:T(8,128)(2,1)S(1)}, u32[]{:S(2)}, u32[]{:S(2)}) collective-permute-start(bf16[127,1024]{1,0:T(8,128)(2,1)S(1)} %slice.93), channel_id=1, source_target_pairs={{0,8},{8,16},{16,24},{24,32},{32,40},{40,48},{48,56},{56,64},{64,7... | collective-permute-start | bytes 780296 | tf_op jit(solution)/shard_map/ppermute | solution.py:10
  18.3 2.2 %slice-start = ((bf16[32896,64]{0,1:T(8,128)(2,1)}), bf16[32768,64]{0,1:T(8,128)(2,1)S(1)}, s32[]{:S(2)}) async-start(bf16[32896,64]{0,1:T(8,128)(2,1)} %tile.10), calls=%async_computation.1 | async-start | bytes 8388608 | tf_op jit(solution)/shard_map/slice | solution.py:23
  20.5 3.0 %copy-start = (f32[16,1024]{1,0:T(8,128)S(1)}, f32[16,1024]{1,0:T(8,128)}, u32[]{:S(2)}) copy-start(f32[16,1024]{1,0:T(8,128)} %param.17) | copy-start | bytes 196612
  20.5 3.2 %copy-start.6 = (f32[16,1024]{1,0:T(8,128)S(1)}, f32[16,1024]{1,0:T(8,128)}, u32[]{:S(2)}) copy-start(f32[16,1024]{1,0:T(8,128)} %param.18) | copy-start | bytes 196612
  23.5 4.2 %copy-start.4 = (bf16[128,1024]{1,0:T(8,128)(2,1)S(1)}, bf16[128,1024]{1,0:T(8,128)(2,1)}, u32[]{:S(2)}) copy-start(bf16[128,1024]{1,0:T(8,128)(2,1)} %param.15) | copy-start | bytes 786436
  23.5 4.2 %copy-start.5 = (bf16[128,1024]{1,0:T(8,128)(2,1)S(1)}, bf16[128,1024]{1,0:T(8,128)(2,1)}, u32[]{:S(2)}) copy-start(bf16[128,1024]{1,0:T(8,128)(2,1)} %param.11) | copy-start | bytes 786436
  44.6 2.6 %copy-start.1 = (f32[4,16,1024]{2,1,0:T(8,128)}, f32[4,16,1024]{2,1,0:T(8,128)S(1)}, u32[]{:S(2)}) copy-start(f32[4,16,1024]{2,1,0:T(8,128)S(1)} %pad.24) | copy-start | bytes 786436
  47.2 107.9 %all-to-all-start = ((f32[64,1,16,1024]{3,2,1,0:T(8,128)}), f32[64,1,16,1024]{3,2,1,0:T(8,128)}, u32[]{:S(2)}, u32[]{:S(2)}) async-start(f32[64,1,16,1024]{3,2,1,0:T(8,128)} %stack.2), calls=%async_computation | async-start | bytes 8388608 | tf_op jit(solution)/shard_map/all_to_all | solution.py:86
  178.5 2.9 %copy-start.2 = (bf16[128,1024]{1,0:T(8,128)(2,1)S(1)}, bf16[128,1024]{1,0:T(8,128)(2,1)}, u32[]{:S(2)}) copy-start(bf16[128,1024]{1,0:T(8,128)(2,1)} %param.14) | copy-start | bytes 786436
  178.5 2.9 %copy-start.3 = (bf16[128,1024]{1,0:T(8,128)(2,1)S(1)}, bf16[128,1024]{1,0:T(8,128)(2,1)}, u32[]{:S(2)}) copy-start(bf16[128,1024]{1,0:T(8,128)(2,1)} %param.10) | copy-start | bytes 786436
  178.5 26.3 %copy-start.7 = (f32[1024]{0:T(1024)S(1)}, f32[1024]{0:T(1024)}, u32[]{:S(2)}) copy-start(f32[1024]{0:T(1024)} %param.19) | copy-start | bytes 12292
